TPU v7x, 512 devices: a whole 4x4x16 slice. The times are simulated.
512 devices in a mesh: row: 8 (over x, y_lo), col: 16 (over z), dp: 4 (over y_hi, core).
Axes of the slice: x: 4, y: 4 (y_hi: 2, y_lo: 2; y = y_hi * 2 + y_lo), z: 16, core: 2. Of those that a mesh axis runs over, the one named last changes fastest.
Arguments:
- tokens: bfloat16 [512, 16384], P('dp', 'col'), may hold values from -6 to 6
- block_values: bfloat16 [8, 16, 32, 128, 128], P('row', 'col'), may hold values from -0.21875 to 0.21875
- block_index: int32 [8, 16, 2, 32], P('row', 'col'), may hold values from 0 to 31, as said below
- block_count: int32 [8, 16], P('row', 'col'), may hold values from 4 to 32, as said below
- grad_hidden: bfloat16 [512, 32768], P('dp', ('row', 'col')), may hold values from -3 to 3
Outputs:
- hidden: bfloat16 [512, 32768], P('dp', ('row', 'col'))
- grad_tokens: bfloat16 [512, 16384], P('dp', ('col', 'row'))
- grad_blocks: bfloat16 [8, 16, 32, 128, 128], P('row', 'col', 'dp')
Inputs may be any that keep to these rules, and one draw needn't show every extreme that they name: block_index[r, c, 0, s] is a block row below 32 and block_index[r, c, 1, s] a block column below 8 inside cell (r, c); the live slots of a cell name distinct positions; slots at or past block_count[r, c] are unused. `block_count`: some cell holds exactly 32 live slots in every draw.
All inputs are finite; a program needn't handle non-finite values.
Results may differ from a plain program's by a relative error of at most 0.017.
Values may be sent and summed in bfloat16 or wider, within the bound.
No kernel may reach another device: no remote copies, remote signals or barrier semaphores. Data moves between devices by JAX's collectives and lax.ppermute only.
A program may use at most 64 MiB of HBM per device.

v0:
```python
import jax
import jax.numpy as jnp
from jax import lax
from jax.sharding import PartitionSpec as P

grad_scale = 0.0625


def masked_total(make_terms, segment_ids, live_slots, segments):
    capacity = segment_ids.shape[0]
    slot_terms = jnp.where(live_slots[:, None, None], make_terms(0, capacity), 0.0)
    return jax.ops.segment_sum(slot_terms, segment_ids, num_segments=segments)


def local(tokens, block_values, block_index, block_count, grad_hidden):
    weight_blocks = block_values[0, 0]
    block_rows = block_index[0, 0, 0]
    block_cols = block_index[0, 0, 1]
    live_count = block_count[0, 0]
    capacity = weight_blocks.shape[0]
    block_size = weight_blocks.shape[1]
    token_count = tokens.shape[0]
    col_blocks = tokens.shape[1] // block_size
    piece_blocks = grad_hidden.shape[1] // block_size
    col_devices = lax.axis_size("col")
    dp_devices = lax.axis_size("dp")
    row_blocks = piece_blocks * col_devices
    live_slots = jnp.arange(capacity) < live_count
    token_blocks = tokens.reshape(token_count, col_blocks, block_size)

    def forward_terms(first_slot, number):
        chosen = jnp.take(token_blocks, block_cols, axis=1)
        return jnp.einsum("tsm,snm->stn", chosen, weight_blocks, preferred_element_type=jnp.float32)

    hidden_blocks = masked_total(forward_terms, block_rows, live_slots, row_blocks)
    hidden_part = hidden_blocks.transpose(1, 0, 2).reshape(token_count, row_blocks * block_size)
    hidden = lax.psum_scatter(
        hidden_part.astype(jnp.bfloat16), "col", scatter_dimension=1, tiled=True
    )
    dp_index = lax.axis_index("dp")
    owned_slots = capacity // dp_devices
    own_first = dp_index * owned_slots
    own_live = lax.dynamic_slice_in_dim(live_slots, own_first, owned_slots)
    local_rows = lax.all_gather(grad_hidden, "col", axis=1, tiled=True).reshape(
        token_count, row_blocks, block_size
    )

    def grad_terms(first_slot, number):
        picked = jnp.take(local_rows, block_rows, axis=1)
        return jnp.einsum("tsn,snm->stm", picked, weight_blocks, preferred_element_type=jnp.float32)

    grad_pick = jnp.take(local_rows, block_rows, axis=1)
    token_pick = jnp.take(token_blocks, block_cols, axis=1)
    slot_partial = jnp.einsum(
        "tsn,tsm->snm", grad_pick, token_pick, preferred_element_type=jnp.float32
    )
    weight_sums = lax.psum_scatter(
        slot_partial.astype(jnp.bfloat16), "dp", scatter_dimension=0, tiled=True
    ).astype(jnp.float32)
    feature_blocks = masked_total(grad_terms, block_cols, live_slots, col_blocks)
    feature_part = feature_blocks.transpose(1, 0, 2).reshape(token_count, col_blocks * block_size)
    grad_tokens = lax.psum_scatter(
        feature_part.astype(jnp.bfloat16), "row", scatter_dimension=1, tiled=True
    )
    grad_blocks = jnp.where(own_live[:, None, None], weight_sums * grad_scale, 0.0).astype(
        jnp.bfloat16
    )
    return (hidden, grad_tokens, grad_blocks[None, None])


def solution(mesh):
    in_specs = (
        P("dp", "col"),
        P("row", "col", None, None, None),
        P("row", "col", None, None),
        P("row", "col"),
        P("dp", ("row", "col")),
    )
    out_specs = (
        P("dp", ("row", "col")),
        P("dp", ("col", "row")),
        P("row", "col", "dp", None, None),
    )
    return jax.shard_map(local, mesh=mesh, in_specs=in_specs, out_specs=out_specs, check_vma=False)
```

profile of v0, /device:TPU:1, one launch (start us, length us, event | category | flops | bytes accessed | tf_op | source)
XLA Modules:
  0.0 260.6 jit_solution(12291143587485037593)
XLA Ops:
  7.2 0.0 copy-start
  7.2 0.0 copy-start.4
  7.2 0.0 all-gather.2.cloned.1.call-start
  7.2 1.6 copy.17
  8.9 0.0 all-gather.2.cloned.1.call-update
  8.9 0.0 reduce-scatter.4.cloned.1.call-start
  9.6 1.1 copy.14
  10.7 0.2 copy.15
  10.9 0.8 compare_and_fusion
  11.7 0.7 gather_fusion
  12.5 0.0 copy-start.1
  12.5 0.0 copy-done.4
  12.5 0.0 copy-done
  12.5 2.2 convolution_select_fusion.1
  14.7 0.0 copy-done.1
  14.8 0.2 broadcast_in_dim.54
  15.0 4.7 %scatter_fusion = f32[32,128,128]{2,1,0:T(8,128)S(1)} fusion(f32[32,128,128]{2,1,0:T(8,128)S(1)} %broadcast_in_dim.54, s32[32]{0:T(128)S(1)} %get-tuple-element.18, f32[32,128,128]{2,1,0:T(8,128)} %convolution_select_fusion.1), kind=kCustom, calls=%fused_computation.2 | custom fusion | flops 524288 | bytes 6291584 | tf_op jit(solution)/shard_map/scatter-add | solution.py:12
  19.7 1.1 convert_bitcast_fusion
  20.8 2.3 copy.16
  23.1 0.0 reduce-scatter.4.cloned.1.call-update
  23.1 0.0 reduce-scatter.6.cloned.1.call-start
  23.1 54.4 %all-gather.2.cloned.1.call-done = bf16[128,4096]{0,1:T(8,128)(2,1)} async-done(((bf16[128,256]{0,1:T(8,128)(2,1)}), bf16[128,4096]{0,1:T(8,128)(2,1)}) %all-gather.2.cloned.1.call-update) | async-done | bytes 1048592 | tf_op jit(solution)/shard_map/all_gather | solution.py:44
  77.6 1.6 copy.18
  79.2 0.7 gather_fusion.1
  80.0 0.0 copy-start.3
  80.0 1.8 convolution_select_fusion
  81.8 0.0 copy-done.3
  81.9 0.0 copy-start.2
  81.9 4.7 %scatter_fusion.1 = f32[8,128,128]{2,1,0:T(8,128)S(1)} fusion(f32[8,128,128]{2,1,0:T(8,128)S(1)} %broadcast_in_dim.56, s32[32]{0:T(128)S(1)} %get-tuple-element.17, f32[32,128,128]{2,1,0:T(8,128)} %convolution_select_fusion), kind=kCustom, calls=%fused_computation.3 | custom fusion | flops 524288 | bytes 6291584 | tf_op jit(solution)/shard_map/scatter-add | solution.py:12
  86.6 0.9 copy.19
  87.4 0.0 reduce-scatter.6.cloned.1.call-update
  87.5 0.0 reduce-scatter.8.cloned.1.call-start
  87.5 0.0 copy-done.2
  87.5 2.8 %convolution_convert_fusion = bf16[32,128,128]{2,1,0:T(8,128)(2,1)} fusion(bf16[32,128,128]{2,1,0:T(8,128)(2,1)S(1)} %copy-done.2, pred[32]{0:T(512)(128)(4,1)S(1)} %get-tuple-element.15, bf16[32,128,128]{2,1,0:T(8,128)(2,1)} %copy-done.3, pred[32]{0:T(512)(128)(4,1)S(1)} %get-tuple-element.11), kind=kOutput, calls=%fused_computation.6 | convolution fusion | flops 135790592 | bytes 3145792 | tf_op jit(solution)/shard_map/tsn,tsm->snm/dot_general | solution.py:54
  90.3 0.0 reduce-scatter.8.cloned.1.call-update
  90.3 0.1 dynamic_slice.3
  90.4 56.6 %reduce-scatter.4.cloned.1.call-done = bf16[128,256]{0,1:T(8,128)(2,1)} async-done(((bf16[128,4096]{0,1:T(8,128)(2,1)}), bf16[128,256]{0,1:T(8,128)(2,1)}) %reduce-scatter.4.cloned.1.call-update) | async-done | bytes 65552 | tf_op jit(solution)/shard_map/reduce_scatter | solution.py:37
  147.0 1.6 copy.21
  148.6 49.5 %reduce-scatter.6.cloned.1.call-done = bf16[128,128]{0,1:T(8,128)(2,1)} async-done(((bf16[128,1024]{0,1:T(8,128)(2,1)}), bf16[128,128]{0,1:T(8,128)(2,1)}) %reduce-scatter.6.cloned.1.call-update) | async-done | bytes 32784 | tf_op jit(solution)/shard_map/reduce_scatter | solution.py:62
  198.0 1.5 copy.22
  199.5 52.8 %reduce-scatter.8.cloned.1.call-done = bf16[8,128,128]{2,1,0:T(8,128)(2,1)} async-done(((bf16[32,128,128]{2,1,0:T(8,128)(2,1)}), bf16[8,128,128]{2,1,0:T(8,128)(2,1)}) %reduce-scatter.8.cloned.1.call-update) | async-done | bytes 262160 | tf_op jit(solution)/shard_map/reduce_scatter | solution.py:57
  252.3 1.8 fusion.6
  (5 shorter events, 0.1 us)
Async XLA Ops:
  7.2 5.3 %copy-start = (bf16[1,1,32,128,128]{4,3,2,1,0:T(8,128)(2,1)S(1)}, bf16[1,1,32,128,128]{4,3,2,1,0:T(8,128)(2,1)}, u32[]{:S(2)}) copy-start(bf16[1,1,32,128,128]{4,3,2,1,0:T(8,128)(2,1)} %param.10) | copy-start | bytes 3145732
  7.2 5.3 %copy-start.4 = (s32[1,1,2,32]{3,2,1,0:T(2,128)S(1)}, s32[1,1,2,32]{3,2,1,0:T(2,128)}, u32[]{:S(2)}) copy-start(s32[1,1,2,32]{3,2,1,0:T(2,128)} %param.11) | copy-start | bytes 772
  7.2 70.4 %all-gather.2.cloned.1.call-start = ((), (), s32[]{:S(2)}) async-start(), calls=%async_computation.4 | async-start | bytes 1114112 | tf_op jit(solution)/shard_map/all_gather | solution.py:44
  8.9 138.1 %reduce-scatter.4.cloned.1.call-start = ((), (), s32[]{:S(2)}) async-start(), calls=%async_computation.3 | async-start | bytes 1114112 | tf_op jit(solution)/shard_map/reduce_scatter | solution.py:37
  12.5 2.3 copy-start.1
  23.1 174.9 %reduce-scatter.6.cloned.1.call-start = ((), (), s32[]{:S(2)}) async-start(), calls=%async_computation.5 | async-start | bytes 294912 | tf_op jit(solution)/shard_map/reduce_scatter | solution.py:62
  80.0 1.8 copy-start.3
  81.9 5.7 %copy-start.2 = (bf16[32,128,128]{2,1,0:T(8,128)(2,1)S(1)}, bf16[32,128,128]{2,1,0:T(8,128)(2,1)}, u32[]{:S(2)}) copy-start(bf16[32,128,128]{2,1,0:T(8,128)(2,1)} %copy-done.1) | copy-start | bytes 3145732
  87.5 164.9 %reduce-scatter.8.cloned.1.call-start = ((), (), s32[]{:S(2)}) async-start(), calls=%async_computation.6 | async-start | bytes 1310720 | tf_op jit(solution)/shard_map/reduce_scatter | solution.py:57
Sparse Core Ops, SparseCore 0:
  10.7 66.8 all-gather.1
  80.4 66.5 reduce-scatter.3
  150.6 47.4 reduce-scatter.5
  200.9 51.3 reduce-scatter.7
where the time goes:
time: 261 us
  waiting for transfers between devices  213 us (82%)
  between operations  14.6 us (6%)
  other arithmetic  13.1 us (5%)
  local copies, waits for them, and re-layouts  12.6 us (5%)
  matrix products  6.87 us (3%)
    reduce_scatter x1, waiting for transfers between devices, local(): lax.psum_scatter(hidden_part.astype(jnp.bfloat16), 'col', scatter_dimensi...  56.6 us
    all_gather x1, waiting for transfers between devices, local(): lax.all_gather(grad_hidden, 'col', axis=1, tiled=True)  54.4 us
    reduce_scatter x1, waiting for transfers between devices, local(): lax.psum_scatter(slot_partial.astype(jnp.bfloat16), 'dp', scatter_dimensi...  52.8 us
    reduce_scatter x1, waiting for transfers between devices, local(): lax.psum_scatter(feature_part.astype(jnp.bfloat16), 'row', scatter_dimens...  49.5 us
    scatter-add x2, other arithmetic, masked_total(): return jax.ops.segment_sum(slot_terms, segment_ids, num_segments=segments)  9.33 us
    unnamed x14, local copies, waits for them, and re-layouts  5.84 us
  transfers between devices with their start and end apart: 4, of which 4 were waited for; matrix products, arithmetic and copies ran while one was open for 11% of the time, Pallas kernels for 0%

commit v1 on v0

--- a/solution.py
+++ b/solution.py
@@ -4,6 +4,28 @@
 from jax.sharding import PartitionSpec as P
 
 grad_scale = 0.0625
+
+
+def in_order(blocks, dim):
+    blocks = jnp.moveaxis(blocks, 0, dim)
+    lengths = blocks.shape
+    return blocks.reshape(*lengths[:dim], lengths[dim] * lengths[dim + 1], *lengths[dim + 2 :])
+
+
+def gather_around(value, axis, dim):
+    size = lax.axis_size(axis)
+    pairs = [(i, (i + 1) % size) for i in range(size)]
+    back = [(b, a) for a, b in pairs]
+    lower, upper = ([], [])
+    for step in range(size - 1):
+        if step % 2 == 0:
+            lower.append(lax.ppermute(lower[-1] if lower else value, axis, pairs))
+        else:
+            upper.append(lax.ppermute(upper[-1] if upper else value, axis, back))
+    blocks = jnp.stack([*lower[::-1], value, *upper])
+    shift = lax.axis_index(axis) - len(lower)
+    blocks = blocks[(jnp.arange(size) - shift) % size]
+    return in_order(blocks, dim)
 
 
 def masked_total(make_terms, segment_ids, live_slots, segments):
@@ -41,9 +63,7 @@
     owned_slots = capacity // dp_devices
     own_first = dp_index * owned_slots
     own_live = lax.dynamic_slice_in_dim(live_slots, own_first, owned_slots)
-    local_rows = lax.all_gather(grad_hidden, "col", axis=1, tiled=True).reshape(
-        token_count, row_blocks, block_size
-    )
+    local_rows = gather_around(grad_hidden, "col", 1).reshape(token_count, row_blocks, block_size)
 
     def grad_terms(first_slot, number):
         picked = jnp.take(local_rows, block_rows, axis=1)

time: 261 us -> 275 us (1.054)
  starting transfers between devices: 0.16 us -> 50.1 us
  waiting for transfers between devices: 213 us -> 164 us
  local copies, waits for them, and re-layouts: 12.6 us -> 27 us
    all_gather x1 -> x0, waiting for transfers between devices: 54.4 us -> none  [local(): lax.all_gather(grad_hidden, 'col', axis=1, tiled=True)]
    ppermute x0 -> x15, starting transfers between devices: none -> 50 us  [the longest x7 32 us: gather_around(): upper.append(lax.ppermute(upper[-1] if upper else value, axis, back))]
    reduce_scatter x1, waiting for transfers between devices: 49.5 us -> 31.7 us  [local(): lax.psum_scatter(feature_part.astype(jnp.bfloat16), 'row', scatter_dimens...]
    ppermute x0 -> x15, waiting for transfers between devices: none -> 9.46 us  [the longest x8 9.45 us: gather_around(): lower.append(lax.ppermute(lower[-1] if lower else value, axis, pairs))]
    reduce_scatter x1, waiting for transfers between devices: 56.6 us -> 65.7 us  [local(): lax.psum_scatter(hidden_part.astype(jnp.bfloat16), 'col', scatter_dimensi...]
    unnamed x14 -> x30, local copies, waits for them, and re-layouts: 5.84 us -> 13.7 us
    reduce_scatter x1, waiting for transfers between devices: 52.8 us -> 56.7 us  [local(): lax.psum_scatter(slot_partial.astype(jnp.bfloat16), 'dp', scatter_dimensi...]
    another operation x0 -> x2, local copies, waits for them, and re-layouts: none -> 2.9 us  [the longest x1 2.27 us: local(): gather_around(grad_hidden, 'col', 1)]
  transfers between devices with their start and end apart: 4 -> 18, of which waited for: 4 -> 4; matrix products, arithmetic and copies ran while one was open for 11% -> 10% of each run, Pallas kernels for 0% -> 0%
where the time goes in v1:
time: 275 us; the launch traced here: 274 us
  waiting for transfers between devices  164 us (60%)
  starting transfers between devices  50.1 us (18%)
  local copies, waits for them, and re-layouts  27 us (10%)
  between operations  14.8 us (5%)
  other arithmetic  13.1 us (5%)
  matrix products  5.6 us (2%)
    reduce_scatter x1, waiting for transfers between devices, local(): lax.psum_scatter(hidden_part.astype(jnp.bfloat16), 'col', scatter_dimensi...  65.7 us
    reduce_scatter x1, waiting for transfers between devices, local(): lax.psum_scatter(slot_partial.astype(jnp.bfloat16), 'dp', scatter_dimensi...  56.7 us
    ppermute x7, starting transfers between devices, gather_around(): upper.append(lax.ppermute(upper[-1] if upper else value, axis, back))  32 us
    reduce_scatter x1, waiting for transfers between devices, local(): lax.psum_scatter(feature_part.astype(jnp.bfloat16), 'row', scatter_dimens...  31.7 us
    ppermute x8, starting transfers between devices, gather_around(): lower.append(lax.ppermute(lower[-1] if lower else value, axis, pairs))  17.9 us
    unnamed x30, local copies, waits for them, and re-layouts  13.7 us
    ppermute x8, waiting for transfers between devices, gather_around(): lower.append(lax.ppermute(lower[-1] if lower else value, axis, pairs))  9.45 us
    scatter-add x2, other arithmetic, masked_total(): return jax.ops.segment_sum(slot_terms, segment_ids, num_segments=segments)  9.33 us
  transfers between devices with their start and end apart: 18, of which 4 were waited for; matrix products, arithmetic and copies ran while one was open for 10% of the time, Pallas kernels for 0%

profile of v1, /device:TPU:1, one launch (start us, length us, event | category | flops | bytes accessed | tf_op | source)
XLA Modules:
  0.0 274.2 jit_solution(7429075071611075907)
XLA Ops:
  7.2 0.0 copy-start
  7.2 0.0 reduce-scatter.6.cloned.1.call-start
  7.2 4.5 %collective-permute-start = (bf16[128,256]{1,0:T(8,128)(2,1)}, bf16[128,256]{1,0:T(8,128)(2,1)S(1)}, u32[]{:S(2)}, u32[]{:S(2)}) collective-permute-start(bf16[128,256]{1,0:T(8,128)(2,1)} %param.13), channel_id=1, source_target_pairs={{0,4},{4,8},{8,12},{12,16},{16,20},{20,24},{24,28},{28,32},{32,36}... | collective-permute-start | bytes 196616 | tf_op jit(solution)/shard_map/ppermute | solution.py:22
  11.7 9.4 %collective-permute-done = bf16[128,256]{1,0:T(8,128)(2,1)S(1)} collective-permute-done((bf16[128,256]{1,0:T(8,128)(2,1)}, bf16[128,256]{1,0:T(8,128)(2,1)S(1)}, u32[]{:S(2)}, u32[]{:S(2)}) %collective-permute-start) | collective-permute-done | bytes 65568 | tf_op jit(solution)/shard_map/ppermute | solution.py:22
  21.2 1.9 collective-permute-start.1
  23.1 4.6 %collective-permute-start.8 = (bf16[128,256]{1,0:T(8,128)(2,1)}, bf16[128,256]{1,0:T(8,128)(2,1)S(1)}, u32[]{:S(2)}, u32[]{:S(2)}) collective-permute-start(bf16[128,256]{1,0:T(8,128)(2,1)} %param.13), channel_id=1, source_target_pairs={{4,0},{8,4},{12,8},{16,12},{20,16},{24,20},{28,24},{32,28},{36,32}... | collective-permute-start | bytes 196616 | tf_op jit(solution)/shard_map/ppermute | solution.py:24
  27.7 1.9 collective-permute-start.2
  29.6 0.8 compare_and_fusion
  30.4 4.6 %collective-permute-start.9 = (bf16[128,256]{1,0:T(8,128)(2,1)S(1)}, bf16[128,256]{1,0:T(8,128)(2,1)S(1)}, u32[]{:S(2)}, u32[]{:S(2)}) collective-permute-start(bf16[128,256]{1,0:T(8,128)(2,1)S(1)} %collective-permute-done.8), channel_id=1, source_target_pairs={{4,0},{8,4},{12,8},{16,12},{20,16},{24,20},{28,24},{32,28},{36,32}... | collective-permute-start | bytes 196616 | tf_op jit(solution)/shard_map/ppermute | solution.py:24
  35.0 1.9 collective-permute-start.3
  36.9 0.8 slice_bitcast_fusion
  38.3 1.1 copy.15
  39.5 0.2 copy.16
  39.7 4.6 %collective-permute-start.10 = (bf16[128,256]{1,0:T(8,128)(2,1)S(1)}, bf16[128,256]{1,0:T(8,128)(2,1)S(1)}, u32[]{:S(2)}, u32[]{:S(2)}) collective-permute-start(bf16[128,256]{1,0:T(8,128)(2,1)S(1)} %collective-permute-done.9), channel_id=1, source_target_pairs={{4,0},{8,4},{12,8},{16,12},{20,16},{24,20},{28,24},{32,28},{36,32}... | collective-permute-start | bytes 196616 | tf_op jit(solution)/shard_map/ppermute | solution.py:24
  44.3 1.9 collective-permute-start.4
  46.2 0.7 gather_fusion.1
  47.0 4.6 %collective-permute-start.11 = (bf16[128,256]{1,0:T(8,128)(2,1)S(1)}, bf16[128,256]{1,0:T(8,128)(2,1)S(1)}, u32[]{:S(2)}, u32[]{:S(2)}) collective-permute-start(bf16[128,256]{1,0:T(8,128)(2,1)S(1)} %collective-permute-done.10), channel_id=1, source_target_pairs={{4,0},{8,4},{12,8},{16,12},{20,16},{24,20},{28,24},{32,28},{36,32}... | collective-permute-start | bytes 196616 | tf_op jit(solution)/shard_map/ppermute | solution.py:24
  51.6 1.9 collective-permute-start.5
  53.5 4.6 %collective-permute-start.12 = (bf16[128,256]{1,0:T(8,128)(2,1)S(1)}, bf16[128,256]{1,0:T(8,128)(2,1)S(1)}, u32[]{:S(2)}, u32[]{:S(2)}) collective-permute-start(bf16[128,256]{1,0:T(8,128)(2,1)S(1)} %collective-permute-done.11), channel_id=1, source_target_pairs={{4,0},{8,4},{12,8},{16,12},{20,16},{24,20},{28,24},{32,28},{36,32}... | collective-permute-start | bytes 196616 | tf_op jit(solution)/shard_map/ppermute | solution.py:24
  58.1 1.9 collective-permute-start.6
  60.1 4.6 %collective-permute-start.13 = (bf16[128,256]{1,0:T(8,128)(2,1)S(1)}, bf16[128,256]{1,0:T(8,128)(2,1)S(1)}, u32[]{:S(2)}, u32[]{:S(2)}) collective-permute-start(bf16[128,256]{1,0:T(8,128)(2,1)S(1)} %collective-permute-done.12), channel_id=1, source_target_pairs={{4,0},{8,4},{12,8},{16,12},{20,16},{24,20},{28,24},{32,28},{36,32}... | collective-permute-start | bytes 196616 | tf_op jit(solution)/shard_map/ppermute | solution.py:24
  64.7 1.9 collective-permute-start.7
  66.6 4.6 %collective-permute-start.14 = (bf16[128,256]{1,0:T(8,128)(2,1)S(1)}, bf16[128,256]{1,0:T(8,128)(2,1)S(1)}, u32[]{:S(2)}, u32[]{:S(2)}) collective-permute-start(bf16[128,256]{1,0:T(8,128)(2,1)S(1)} %collective-permute-done.13), channel_id=1, source_target_pairs={{4,0},{8,4},{12,8},{16,12},{20,16},{24,20},{28,24},{32,28},{36,32}... | collective-permute-start | bytes 196616 | tf_op jit(solution)/shard_map/ppermute | solution.py:24
  71.2 0.6 bitcast_dynamic-update-slice_fusion.15
  71.9 0.6 bitcast_dynamic-update-slice_fusion.14
  72.5 0.6 bitcast_dynamic-update-slice_fusion.13
  73.1 0.6 bitcast_dynamic-update-slice_fusion.12
  73.7 0.6 bitcast_dynamic-update-slice_fusion.11
  74.4 0.6 bitcast_dynamic-update-slice_fusion.10
  75.0 0.6 bitcast_dynamic-update-slice_fusion.9
  75.6 0.6 bitcast_dynamic-update-slice_fusion.8
  76.3 0.6 bitcast_dynamic-update-slice_fusion.7
  76.9 0.6 bitcast_dynamic-update-slice_fusion.6
  77.5 0.6 bitcast_dynamic-update-slice_fusion.5
  78.2 0.6 bitcast_dynamic-update-slice_fusion.4
  78.8 0.6 bitcast_dynamic-update-slice_fusion.3
  79.4 0.6 bitcast_dynamic-update-slice_fusion.2
  80.1 0.6 bitcast_dynamic-update-slice_fusion.1
  80.7 0.6 bitcast_dynamic-update-slice_fusion
  81.3 1.8 gather_fusion
  83.2 1.3 copy.18
  84.5 2.3 copy.19
  86.8 2.0 gather_fusion.2
  88.8 1.8 convolution_select_fusion
  90.6 4.7 %scatter_fusion.1 = f32[8,128,128]{2,1,0:T(8,128)S(1)} fusion(f32[8,128,128]{2,1,0:T(8,128)S(1)} %broadcast_in_dim.57, s32[32]{0:T(128)S(1)} %get-tuple-element.17, f32[32,128,128]{2,1,0:T(8,128)} %convolution_select_fusion), kind=kCustom, calls=%fused_computation.4 | custom fusion | flops 524288 | bytes 6291584 | tf_op jit(solution)/shard_map/scatter-add | solution.py:34
  95.4 0.9 copy.20
  96.2 0.0 reduce-scatter.6.cloned.1.call-update
  96.2 0.0 reduce-scatter.4.cloned.1.call-start
  96.3 2.2 convolution_select_fusion.1
  98.5 0.2 broadcast_in_dim.55
  98.7 4.7 %scatter_fusion = f32[32,128,128]{2,1,0:T(8,128)S(1)} fusion(f32[32,128,128]{2,1,0:T(8,128)S(1)} %broadcast_in_dim.55, s32[32]{0:T(128)S(1)} %get-tuple-element.18, f32[32,128,128]{2,1,0:T(8,128)} %convolution_select_fusion.1), kind=kCustom, calls=%fused_computation.3 | custom fusion | flops 524288 | bytes 6291584 | tf_op jit(solution)/shard_map/scatter-add | solution.py:34
  103.4 1.2 convert_bitcast_fusion
  104.6 2.4 copy.17
  107.0 0.0 reduce-scatter.4.cloned.1.call-update
  107.0 0.0 reduce-scatter.8.cloned.1.call-start
  107.1 1.6 convolution_convert_fusion
  108.7 0.0 reduce-scatter.8.cloned.1.call-update
  108.7 0.1 dynamic_slice.3
  108.8 31.7 %reduce-scatter.6.cloned.1.call-done = bf16[128,128]{0,1:T(8,128)(2,1)} async-done(((bf16[128,1024]{0,1:T(8,128)(2,1)}), bf16[128,128]{0,1:T(8,128)(2,1)}) %reduce-scatter.6.cloned.1.call-update) | async-done | bytes 32784 | tf_op jit(solution)/shard_map/reduce_scatter | solution.py:82
  140.5 1.5 copy.23
  142.0 65.7 %reduce-scatter.4.cloned.1.call-done = bf16[128,256]{0,1:T(8,128)(2,1)} async-done(((bf16[128,4096]{0,1:T(8,128)(2,1)}), bf16[128,256]{0,1:T(8,128)(2,1)}) %reduce-scatter.4.cloned.1.call-update) | async-done | bytes 65552 | tf_op jit(solution)/shard_map/reduce_scatter | solution.py:59
  207.6 1.6 copy.22
  209.2 56.7 %reduce-scatter.8.cloned.1.call-done = bf16[8,128,128]{2,1,0:T(8,128)(2,1)} async-done(((bf16[32,128,128]{2,1,0:T(8,128)(2,1)}), bf16[8,128,128]{2,1,0:T(8,128)(2,1)}) %reduce-scatter.8.cloned.1.call-update) | async-done | bytes 262160 | tf_op jit(solution)/shard_map/reduce_scatter | solution.py:77
  265.9 1.8 fusion.6
  (31 shorter events, 0.2 us)
Async XLA Ops:
  7.2 81.6 %copy-start = (bf16[1,1,32,128,128]{4,3,2,1,0:T(8,128)(2,1)S(1)}, bf16[1,1,32,128,128]{4,3,2,1,0:T(8,128)(2,1)}, u32[]{:S(2)}) copy-start(bf16[1,1,32,128,128]{4,3,2,1,0:T(8,128)(2,1)} %param.10) | copy-start | bytes 3145732
  7.2 133.3 %reduce-scatter.6.cloned.1.call-start = ((), (), s32[]{:S(2)}) async-start(), calls=%async_computation.4 | async-start | bytes 294912 | tf_op jit(solution)/shard_map/reduce_scatter | solution.py:82
  7.2 13.9 %collective-permute-start = (bf16[128,256]{1,0:T(8,128)(2,1)}, bf16[128,256]{1,0:T(8,128)(2,1)S(1)}, u32[]{:S(2)}, u32[]{:S(2)}) collective-permute-start(bf16[128,256]{1,0:T(8,128)(2,1)} %param.13), channel_id=1, source_target_pairs={{0,4},{4,8},{8,12},{12,16},{16,20},{20,24},{24,28},{28,32},{32,36}... | collective-permute-start | bytes 196616 | tf_op jit(solution)/shard_map/ppermute | solution.py:22
  21.2 6.5 %collective-permute-start.1 = (bf16[128,256]{1,0:T(8,128)(2,1)S(1)}, bf16[128,256]{1,0:T(8,128)(2,1)S(1)}, u32[]{:S(2)}, u32[]{:S(2)}) collective-permute-start(bf16[128,256]{1,0:T(8,128)(2,1)S(1)} %collective-permute-done), channel_id=1, source_target_pairs={{0,4},{4,8},{8,12},{12,16},{16,20},{20,24},{24,28},{28,32},{32,36}... | collective-permute-start | bytes 196616 | tf_op jit(solution)/shard_map/ppermute | solution.py:22
  23.1 7.3 %collective-permute-start.8 = (bf16[128,256]{1,0:T(8,128)(2,1)}, bf16[128,256]{1,0:T(8,128)(2,1)S(1)}, u32[]{:S(2)}, u32[]{:S(2)}) collective-permute-start(bf16[128,256]{1,0:T(8,128)(2,1)} %param.13), channel_id=1, source_target_pairs={{4,0},{8,4},{12,8},{16,12},{20,16},{24,20},{28,24},{32,28},{36,32}... | collective-permute-start | bytes 196616 | tf_op jit(solution)/shard_map/ppermute | solution.py:24
  27.7 7.3 %collective-permute-start.2 = (bf16[128,256]{1,0:T(8,128)(2,1)S(1)}, bf16[128,256]{1,0:T(8,128)(2,1)S(1)}, u32[]{:S(2)}, u32[]{:S(2)}) collective-permute-start(bf16[128,256]{1,0:T(8,128)(2,1)S(1)} %collective-permute-done.1), channel_id=1, source_target_pairs={{0,4},{4,8},{8,12},{12,16},{16,20},{20,24},{24,28},{28,32},{32,36}... | collective-permute-start | bytes 196616 | tf_op jit(solution)/shard_map/ppermute | solution.py:22
  30.4 9.3 %collective-permute-start.9 = (bf16[128,256]{1,0:T(8,128)(2,1)S(1)}, bf16[128,256]{1,0:T(8,128)(2,1)S(1)}, u32[]{:S(2)}, u32[]{:S(2)}) collective-permute-start(bf16[128,256]{1,0:T(8,128)(2,1)S(1)} %collective-permute-done.8), channel_id=1, source_target_pairs={{4,0},{8,4},{12,8},{16,12},{20,16},{24,20},{28,24},{32,28},{36,32}... | collective-permute-start | bytes 196616 | tf_op jit(solution)/shard_map/ppermute | solution.py:24
  35.0 9.3 %collective-permute-start.3 = (bf16[128,256]{1,0:T(8,128)(2,1)S(1)}, bf16[128,256]{1,0:T(8,128)(2,1)S(1)}, u32[]{:S(2)}, u32[]{:S(2)}) collective-permute-start(bf16[128,256]{1,0:T(8,128)(2,1)S(1)} %collective-permute-done.2), channel_id=1, source_target_pairs={{0,4},{4,8},{8,12},{12,16},{16,20},{20,24},{24,28},{28,32},{32,36}... | collective-permute-start | bytes 196616 | tf_op jit(solution)/shard_map/ppermute | solution.py:22
  38.3 38.0 %copy-start.5 = (bf16[128,256]{1,0:T(8,128)(2,1)S(1)}, bf16[128,256]{1,0:T(8,128)(2,1)}, u32[]{:S(2)}) copy-start(bf16[128,256]{1,0:T(8,128)(2,1)} %param.13) | copy-start | bytes 196612
  39.7 7.3 %collective-permute-start.10 = (bf16[128,256]{1,0:T(8,128)(2,1)S(1)}, bf16[128,256]{1,0:T(8,128)(2,1)S(1)}, u32[]{:S(2)}, u32[]{:S(2)}) collective-permute-start(bf16[128,256]{1,0:T(8,128)(2,1)S(1)} %collective-permute-done.9), channel_id=1, source_target_pairs={{4,0},{8,4},{12,8},{16,12},{20,16},{24,20},{28,24},{32,28},{36,32}... | collective-permute-start | bytes 196616 | tf_op jit(solution)/shard_map/ppermute | solution.py:24
  44.3 7.3 %collective-permute-start.4 = (bf16[128,256]{1,0:T(8,128)(2,1)S(1)}, bf16[128,256]{1,0:T(8,128)(2,1)S(1)}, u32[]{:S(2)}, u32[]{:S(2)}) collective-permute-start(bf16[128,256]{1,0:T(8,128)(2,1)S(1)} %collective-permute-done.3), channel_id=1, source_target_pairs={{0,4},{4,8},{8,12},{12,16},{16,20},{20,24},{24,28},{28,32},{32,36}... | collective-permute-start | bytes 196616 | tf_op jit(solution)/shard_map/ppermute | solution.py:22
  47.0 49.3 %copy-start.1 = (bf16[32,128,128]{2,1,0:T(8,128)(2,1)}, bf16[32,128,128]{2,1,0:T(8,128)(2,1)S(1)}, u32[]{:S(2)}) copy-start(bf16[32,128,128]{2,1,0:T(8,128)(2,1)S(1)} %gather_fusion.1) | copy-start | bytes 3145732
  47.0 6.5 %collective-permute-start.11 = (bf16[128,256]{1,0:T(8,128)(2,1)S(1)}, bf16[128,256]{1,0:T(8,128)(2,1)S(1)}, u32[]{:S(2)}, u32[]{:S(2)}) collective-permute-start(bf16[128,256]{1,0:T(8,128)(2,1)S(1)} %collective-permute-done.10), channel_id=1, source_target_pairs={{4,0},{8,4},{12,8},{16,12},{20,16},{24,20},{28,24},{32,28},{36,32}... | collective-permute-start | bytes 196616 | tf_op jit(solution)/shard_map/ppermute | solution.py:24
  51.6 6.5 %collective-permute-start.5 = (bf16[128,256]{1,0:T(8,128)(2,1)S(1)}, bf16[128,256]{1,0:T(8,128)(2,1)S(1)}, u32[]{:S(2)}, u32[]{:S(2)}) collective-permute-start(bf16[128,256]{1,0:T(8,128)(2,1)S(1)} %collective-permute-done.4), channel_id=1, source_target_pairs={{0,4},{4,8},{8,12},{12,16},{16,20},{20,24},{24,28},{28,32},{32,36}... | collective-permute-start | bytes 196616 | tf_op jit(solution)/shard_map/ppermute | solution.py:22
  53.5 6.5 %collective-permute-start.12 = (bf16[128,256]{1,0:T(8,128)(2,1)S(1)}, bf16[128,256]{1,0:T(8,128)(2,1)S(1)}, u32[]{:S(2)}, u32[]{:S(2)}) collective-permute-start(bf16[128,256]{1,0:T(8,128)(2,1)S(1)} %collective-permute-done.11), channel_id=1, source_target_pairs={{4,0},{8,4},{12,8},{16,12},{20,16},{24,20},{28,24},{32,28},{36,32}... | collective-permute-start | bytes 196616 | tf_op jit(solution)/shard_map/ppermute | solution.py:24
  58.1 6.5 %collective-permute-start.6 = (bf16[128,256]{1,0:T(8,128)(2,1)S(1)}, bf16[128,256]{1,0:T(8,128)(2,1)S(1)}, u32[]{:S(2)}, u32[]{:S(2)}) collective-permute-start(bf16[128,256]{1,0:T(8,128)(2,1)S(1)} %collective-permute-done.5), channel_id=1, source_target_pairs={{0,4},{4,8},{8,12},{12,16},{16,20},{20,24},{24,28},{28,32},{32,36}... | collective-permute-start | bytes 196616 | tf_op jit(solution)/shard_map/ppermute | solution.py:22
  60.1 6.5 %collective-permute-start.13 = (bf16[128,256]{1,0:T(8,128)(2,1)S(1)}, bf16[128,256]{1,0:T(8,128)(2,1)S(1)}, u32[]{:S(2)}, u32[]{:S(2)}) collective-permute-start(bf16[128,256]{1,0:T(8,128)(2,1)S(1)} %collective-permute-done.12), channel_id=1, source_target_pairs={{4,0},{8,4},{12,8},{16,12},{20,16},{24,20},{28,24},{32,28},{36,32}... | collective-permute-start | bytes 196616 | tf_op jit(solution)/shard_map/ppermute | solution.py:24
  64.7 6.5 %collective-permute-start.7 = (bf16[128,256]{1,0:T(8,128)(2,1)S(1)}, bf16[128,256]{1,0:T(8,128)(2,1)S(1)}, u32[]{:S(2)}, u32[]{:S(2)}) collective-permute-start(bf16[128,256]{1,0:T(8,128)(2,1)S(1)} %collective-permute-done.6), channel_id=1, source_target_pairs={{0,4},{4,8},{8,12},{12,16},{16,20},{20,24},{24,28},{28,32},{32,36}... | collective-permute-start | bytes 196616 | tf_op jit(solution)/shard_map/ppermute | solution.py:22
  66.6 14.1 %collective-permute-start.14 = (bf16[128,256]{1,0:T(8,128)(2,1)S(1)}, bf16[128,256]{1,0:T(8,128)(2,1)S(1)}, u32[]{:S(2)}, u32[]{:S(2)}) collective-permute-start(bf16[128,256]{1,0:T(8,128)(2,1)S(1)} %collective-permute-done.13), channel_id=1, source_target_pairs={{4,0},{8,4},{12,8},{16,12},{20,16},{24,20},{28,24},{32,28},{36,32}... | collective-permute-start | bytes 196616 | tf_op jit(solution)/shard_map/ppermute | solution.py:24
  88.8 1.8 copy-start.3
  96.2 111.4 %reduce-scatter.4.cloned.1.call-start = ((), (), s32[]{:S(2)}) async-start(), calls=%async_computation.3 | async-start | bytes 1114112 | tf_op jit(solution)/shard_map/reduce_scatter | solution.py:59
  104.6 2.5 copy-start.2
  104.6 2.5 copy-start.4
  107.0 158.9 %reduce-scatter.8.cloned.1.call-start = ((), (), s32[]{:S(2)}) async-start(), calls=%async_computation.5 | async-start | bytes 1310720 | tf_op jit(solution)/shard_map/reduce_scatter | solution.py:77
Sparse Core Ops, SparseCore 0:
  96.4 44.0 reduce-scatter.5
  143.5 64.0 reduce-scatter.3
  210.7 55.1 reduce-scatter.7
